TPU v7x, 1024 devices: a whole 4x8x16 slice. The times are simulated.
1024 devices in a mesh: node: 16 (over z), local: 64 (over x, y, core).
Axes of the slice: x: 4, y: 8, z: 16, core: 2. Of those that a mesh axis runs over, the one named last changes fastest.
Arguments:
- queries: bfloat16 [1024, 128, 576], P(('node', 'local')), may hold values from -64 to 64
- latent_cache: bfloat16 [1024, 320, 576], P(('node', 'local')), may hold values from -8 to 8
- lengths: int32 [1024], P(('node', 'local')), may hold values from 2 to 320, as said below
- moe_rows: bfloat16 [1024, 7168], P(('node', 'local')), may hold values from -6 to 6
- expert_ids: int32 [1024, 8], P(('node', 'local')), may hold values from 0 to 63, as said below
- route_gates: bfloat16 [1024, 8], P(('node', 'local')), may hold values from 0.099609375 to 1
- w_gate: bfloat16 [1024, 64, 7168], P(('node', 'local')), may hold values from -0.0625 to 0.0625
- w_up: bfloat16 [1024, 64, 7168], P(('node', 'local')), may hold values from -0.0625 to 0.0625
- w_down: bfloat16 [1024, 64, 7168], P(('node', 'local')), may hold values from -0.1875 to 0.1875
Outputs:
- context: bfloat16 [1024, 128, 512], P(('node', 'local'))
- moe_out: bfloat16 [1024, 7168], P(('node', 'local'))
Inputs may be any that keep to these rules, and one draw needn't show every extreme that they name: `expert_ids`: each token names 8 distinct experts in 4 groups, 2 in each; expert i is in group i // 4. For every l, among the 16 tokens whose index is l modulo 64, exactly 4 use each group, and each expert of that group is used by exactly 2 of them. `lengths`: some request has all 320 positions valid.
All inputs are finite; a program needn't handle non-finite values.
Results may differ from a plain program's by a relative error of at most 0.017.
Values may be sent and summed in bfloat16 or wider, within the bound.
A program may use at most 32 MiB of HBM per device.

v0:
```python
import jax
import jax.numpy as jnp
from jax import lax
from jax.sharding import PartitionSpec as P

LATENT = 512
E_NODE = 4
PER_GROUP = 2
SLOTS = 2


score_scale = 192.0 ** (-0.5)


def attend(queries, latent_cache, lengths):
    scores = (
        jnp.einsum("rhc,rpc->rhp", queries, latent_cache, preferred_element_type=jnp.float32)
        * score_scale
    )
    positions = jnp.arange(latent_cache.shape[1])
    visible = positions[None, None, :] < lengths[:, None, None]
    scores = jnp.where(visible, scores, -1e30)
    highest = jnp.max(scores, axis=2, keepdims=True)
    weights = jnp.where(visible, jnp.exp(scores - highest), 0.0)
    probabilities = (weights / jnp.sum(weights, axis=2, keepdims=True)).astype(jnp.bfloat16)
    values = latent_cache[:, :, :LATENT]
    return jnp.einsum(
        "rhp,rpc->rhc", probabilities, values, preferred_element_type=jnp.float32
    ).astype(jnp.bfloat16)


def per_device(
    queries, latent_cache, lengths, moe_rows, expert_ids, route_gates, w_gate, w_up, w_down
):
    groups = lax.axis_size("node")
    members = lax.axis_size("local")
    slices = members // E_NODE
    model_width = moe_rows.shape[1]
    context = attend(queries, latent_cache, lengths)
    token_row = moe_rows[0]
    chosen = expert_ids[0]
    gate_values = route_gates[0].astype(jnp.float32)
    in_group = chosen[:, None, None] // E_NODE == jnp.arange(groups)[None, :, None]
    in_expert = chosen[:, None, None] % E_NODE == jnp.arange(E_NODE)[None, None, :]
    group_table = jnp.sum(
        gate_values[:, None, None] * (in_group & in_expert).astype(jnp.float32), axis=0
    )
    wanted = jnp.sum(group_table, axis=1) > 0
    send_rows = jnp.where(wanted[:, None], token_row[None, :], jnp.zeros_like(token_row)[None, :])[
        :, None, :
    ]
    send_gates = group_table.astype(jnp.bfloat16)[:, None, :]
    arrived_rows, arrived_gates = (
        lax.all_to_all(send_rows, "node", split_axis=0, concat_axis=0, tiled=True),
        lax.all_to_all(send_gates, "node", split_axis=0, concat_axis=0, tiled=True),
    )
    slot_gates = arrived_gates[:, 0, :].astype(jnp.float32)
    taken_mask = (slot_gates > 0).astype(jnp.int32)
    standing = jnp.cumsum(taken_mask, axis=0) - 1
    selector = taken_mask[None, :, :] * (standing[None, :, :] == jnp.arange(SLOTS)[:, None, None])
    gathered = jnp.einsum(
        "ksc,sd->ckd",
        selector.astype(jnp.bfloat16),
        arrived_rows[:, 0, :],
        preferred_element_type=jnp.float32,
    ).astype(jnp.bfloat16)
    outgoing = jnp.broadcast_to(gathered[:, None], (E_NODE, slices, SLOTS, model_width)).reshape(
        members, SLOTS, model_width
    )
    incoming = lax.all_to_all(outgoing, "local", split_axis=0, concat_axis=0, tiled=True)
    flat_rows = incoming.reshape(-1, model_width)
    gate_pre = jnp.einsum("rd,hd->rh", flat_rows, w_gate[0], preferred_element_type=jnp.float32)
    up_pre = jnp.einsum("rd,hd->rh", flat_rows, w_up[0], preferred_element_type=jnp.float32)
    hidden = (jax.nn.silu(gate_pre) * up_pre).astype(jnp.bfloat16)
    slice_out = jnp.dot(hidden, w_down[0], preferred_element_type=jnp.float32).astype(jnp.bfloat16)
    returned = lax.all_to_all(
        slice_out.reshape(incoming.shape), "local", split_axis=0, concat_axis=0, tiled=True
    )
    expert_sums = jnp.sum(
        returned.reshape(E_NODE, slices, SLOTS, model_width).astype(jnp.float32), axis=1
    )
    position = jnp.cumsum(taken_mask, axis=1) - 1
    pair_pick = taken_mask[:, None, :] * (
        position[:, None, :] == jnp.arange(PER_GROUP)[None, :, None]
    )
    picked_sums = jnp.einsum(
        "ksc,ckd->scd", selector.astype(jnp.float32), expert_sums, precision=lax.Precision.HIGHEST
    )
    pair_out = jnp.einsum(
        "sjc,scd->sjd", pair_pick.astype(jnp.float32), picked_sums, precision=lax.Precision.HIGHEST
    )
    home_rows = lax.all_to_all(
        pair_out.astype(jnp.bfloat16), "node", split_axis=0, concat_axis=0, tiled=True
    ).astype(pair_out.dtype)
    own_taken = (group_table > 0).astype(jnp.int32)
    own_position = jnp.cumsum(own_taken, axis=1) - 1
    own_pick = own_taken[:, None, :] * (
        own_position[:, None, :] == jnp.arange(PER_GROUP)[None, :, None]
    )
    pair_gates = jnp.sum(group_table[:, None, :] * own_pick.astype(jnp.float32), axis=2)
    node_part = jnp.sum(pair_gates[:, :, None] * home_rows, axis=1).astype(jnp.bfloat16)
    moe_out = jnp.sum(node_part.astype(jnp.float32), axis=0).astype(jnp.bfloat16)
    return (context, moe_out[None, :])


def solution(mesh):
    in_specs = (
        P(("node", "local"), None, None),
        P(("node", "local"), None, None),
        P(("node", "local")),
        P(("node", "local"), None),
        P(("node", "local"), None),
        P(("node", "local"), None),
        P(("node", "local"), None, None),
        P(("node", "local"), None, None),
        P(("node", "local"), None, None),
    )
    out_specs = (P(("node", "local"), None, None), P(("node", "local"), None))
    return jax.shard_map(
        per_device, mesh=mesh, in_specs=in_specs, out_specs=out_specs, check_vma=False
    )
```

profile of v0, /device:TPU:14, one launch (start us, length us, event | category | flops | bytes accessed | tf_op | source)
XLA Modules:
  0.0 220.7 jit_solution(15776696750635629875)
XLA Ops:
  0.6 0.0 copy-start
  0.6 0.7 and_select_fusion.1
  1.4 0.1 iota_compare_fusion
  1.5 0.7 bitcast_convert_fusion
  2.1 0.1 select_reduce_fusion.1
  2.2 0.7 copy.48
  2.9 18.9 %all-to-all-start = ((bf16[16,1,4]{2,1,0:T(2,128)(2,1)}), bf16[16,1,4]{2,1,0:T(2,128)(2,1)S(1)}, u32[]{:S(2)}, u32[]{:S(2)}) async-start(bf16[16,1,4]{2,1,0:T(2,128)(2,1)} %copy.48), calls=%async_computation | async-start | bytes 16384 | tf_op jit(solution)/shard_map/all_to_all | solution.py:55
  21.8 0.8 reduce.6
  22.6 0.4 broadcast_select_fusion
  23.0 0.5 broadcast.274
  23.5 2.0 reduce.7
  25.5 0.8 reshape.317
  26.4 7.8 %all-to-all-done = bf16[16,1,4]{2,1,0:T(2,128)(2,1)S(1)} async-done(((bf16[16,1,4]{2,1,0:T(2,128)(2,1)}), bf16[16,1,4]{2,1,0:T(2,128)(2,1)S(1)}, u32[]{:S(2)}, u32[]{:S(2)}) %all-to-all-start) | async-done | bytes 160 | tf_op jit(solution)/shard_map/all_to_all | solution.py:55
  34.2 4.2 %all-to-all-start.1 = ((bf16[16,2,3584]{2,1,0:T(2,128)(2,1)}), bf16[16,2,3584]{2,1,0:T(2,128)(2,1)S(1)}, u32[]{:S(2)}, u32[]{:S(2)}) async-start(bf16[16,2,3584]{2,1,0:T(2,128)(2,1)} %reshape.317), calls=%async_computation.1 | async-start | bytes 458752 | tf_op jit(solution)/shard_map/all_to_all | solution.py:54
  38.4 0.1 copy.49
  38.5 0.1 copy.50
  38.6 0.1 copy.53
  38.7 16.7 %all-to-all-done.1 = bf16[16,2,3584]{2,1,0:T(2,128)(2,1)S(1)} async-done(((bf16[16,2,3584]{2,1,0:T(2,128)(2,1)}), bf16[16,2,3584]{2,1,0:T(2,128)(2,1)S(1)}, u32[]{:S(2)}, u32[]{:S(2)}) %all-to-all-start.1) | async-done | bytes 229408 | tf_op jit(solution)/shard_map/all_to_all | solution.py:54
  55.4 0.2 reshape.318
  55.5 0.2 fusion
  55.7 0.1 copy.55
  55.8 0.9 broadcast_in_dim.78
  56.8 54.7 %all_to_all.25 = bf16[64,2,7168]{2,1,0:T(2,128)(2,1)} all-to-all(bf16[64,2,7168]{2,1,0:T(2,128)(2,1)S(1)} %bitcast.63), channel_id=1, replica_groups=mesh['node'=16,'local'=64] {'local'}, dimensions={0} | all-to-all | bytes 3670016 | tf_op jit(solution)/shard_map/all_to_all | solution.py:70
  111.5 4.1 %reshape.309 = bf16[128,7168]{1,0:T(8,128)(2,1)S(1)} reshape(bf16[64,2,7168]{2,1,0:T(2,128)(2,1)} %all_to_all.25) | data formatting | bytes 3670016 | tf_op jit(solution)/shard_map/reshape | solution.py:71
  115.6 1.9 fusion.8
  117.5 0.0 copy-done
  117.5 4.6 %convolution_convert_fusion = bf16[128,7168]{1,0:T(8,128)(2,1)} fusion(bf16[128,7168]{1,0:T(8,128)(2,1)S(1)} %reshape.309, bf16[1,64,7168]{2,1,0:T(8,128)(2,1)S(1)} %copy-done, bf16[1,64,7168]{2,1,0:T(8,128)(2,1)} %param.16, f32[128,64]{0,1:T(8,128)S(1)} %fusion.8), kind=kOutput, calls=%fused_computation | convolution fusion | flops 235847680 | bytes 5537792 | tf_op jit(solution)/shard_map/dot_general | solution.py:75
  122.1 4.7 %reshape.310 = bf16[64,2,7168]{2,1,0:T(2,128)(2,1)} reshape(bf16[128,7168]{1,0:T(8,128)(2,1)} %convolution_convert_fusion) | data formatting | bytes 3670016 | tf_op jit(solution)/shard_map/reshape | solution.py:77
  126.9 7.4 %all-to-all-start.3 = ((bf16[64,2,7168]{2,1,0:T(2,128)(2,1)}), bf16[64,2,7168]{2,1,0:T(2,128)(2,1)S(1)}, u32[]{:S(2)}, u32[]{:S(2)}) async-start(bf16[64,2,7168]{2,1,0:T(2,128)(2,1)} %reshape.310), calls=%async_computation.3 | async-start | bytes 3670016 | tf_op jit(solution)/shard_map/all_to_all | solution.py:76
  134.3 0.2 reduce_window_sum.35
  134.5 43.9 %all-to-all-done.3 = bf16[64,2,7168]{2,1,0:T(2,128)(2,1)S(1)} async-done(((bf16[64,2,7168]{2,1,0:T(2,128)(2,1)}), bf16[64,2,7168]{2,1,0:T(2,128)(2,1)S(1)}, u32[]{:S(2)}, u32[]{:S(2)}) %all-to-all-start.3) | async-done | bytes 1835040 | tf_op jit(solution)/shard_map/all_to_all | solution.py:76
  178.4 1.5 convert_reduce_fusion
  179.9 1.6 convolution_bitcast_fusion
  181.6 0.0 copy-start.1
  181.6 0.0 copy-start.2
  181.6 4.5 %convolution_convert_fusion.1 = bf16[16,2,7168]{2,1,0:T(2,128)(2,1)} fusion(f32[16,4,7168]{2,0,1:T(8,128)S(1)} %convolution_bitcast_fusion, s32[16,4]{1,0:T(8,128)S(1)} %copy.50, s32[16,4]{1,0:T(8,128)S(1)} %broadcast_add_fusion.1), kind=kOutput, calls=%fused_computation.2 | convolution fusion | flops 11239808 | bytes 2294272 | tf_op jit(solution)/shard_map/sjc,scd->sjd/dot_general | solution.py:89
  186.1 5.2 %all-to-all-start.4 = ((bf16[16,2,7168]{2,1,0:T(2,128)(2,1)}), bf16[16,2,7168]{2,1,0:T(2,128)(2,1)S(1)}, u32[]{:S(2)}, u32[]{:S(2)}) async-start(bf16[16,2,7168]{2,1,0:T(2,128)(2,1)} %convolution_convert_fusion.1), calls=%async_computation.4 | async-start | bytes 917504 | tf_op jit(solution)/shard_map/all_to_all | solution.py:92
  191.3 0.1 copy.46
  191.4 0.2 reduce_window_sum.32
  192.2 0.1 fusion.28
  192.3 0.0 copy-done.1
  192.3 0.3 fusion.46
  192.6 0.1 fusion.16
  192.7 1.0 fusion.3
  193.8 24.9 %all-to-all-done.4 = bf16[16,2,7168]{2,1,0:T(2,128)(2,1)S(1)} async-done(((bf16[16,2,7168]{2,1,0:T(2,128)(2,1)}), bf16[16,2,7168]{2,1,0:T(2,128)(2,1)S(1)}, u32[]{:S(2)}, u32[]{:S(2)}) %all-to-all-start.4) | async-done | bytes 458784 | tf_op jit(solution)/shard_map/all_to_all | solution.py:92
  218.6 1.3 multiply_reduce_fusion
  220.0 0.1 convert_reduce_fusion.1
  220.0 0.6 broadcast_in_dim.79
  (12 shorter events, 0.1 us)
Async XLA Ops:
  0.6 116.9 %copy-start = (bf16[1,64,7168]{2,1,0:T(8,128)(2,1)S(1)}, bf16[1,64,7168]{2,1,0:T(8,128)(2,1)}, u32[]{:S(2)}) copy-start(bf16[1,64,7168]{2,1,0:T(8,128)(2,1)} %param.17) | copy-start | bytes 2752516
  2.9 31.2 %all-to-all-start = ((bf16[16,1,4]{2,1,0:T(2,128)(2,1)}), bf16[16,1,4]{2,1,0:T(2,128)(2,1)S(1)}, u32[]{:S(2)}, u32[]{:S(2)}) async-start(bf16[16,1,4]{2,1,0:T(2,128)(2,1)} %copy.48), calls=%async_computation | async-start | bytes 16384 | tf_op jit(solution)/shard_map/all_to_all | solution.py:55
  34.2 21.2 %all-to-all-start.1 = ((bf16[16,2,3584]{2,1,0:T(2,128)(2,1)}), bf16[16,2,3584]{2,1,0:T(2,128)(2,1)S(1)}, u32[]{:S(2)}, u32[]{:S(2)}) async-start(bf16[16,2,3584]{2,1,0:T(2,128)(2,1)} %reshape.317), calls=%async_computation.1 | async-start | bytes 458752 | tf_op jit(solution)/shard_map/all_to_all | solution.py:54
  126.9 51.5 %all-to-all-start.3 = ((bf16[64,2,7168]{2,1,0:T(2,128)(2,1)}), bf16[64,2,7168]{2,1,0:T(2,128)(2,1)S(1)}, u32[]{:S(2)}, u32[]{:S(2)}) async-start(bf16[64,2,7168]{2,1,0:T(2,128)(2,1)} %reshape.310), calls=%async_computation.3 | async-start | bytes 3670016 | tf_op jit(solution)/shard_map/all_to_all | solution.py:76
  181.6 10.7 %copy-start.1 = (bf16[1,320,576]{2,1,0:T(8,128)(2,1)S(1)}, bf16[1,320,576]{2,1,0:T(8,128)(2,1)}, u32[]{:S(2)}) copy-start(bf16[1,320,576]{2,1,0:T(8,128)(2,1)} %param.10) | copy-start | bytes 1105924
  181.6 10.7 %copy-start.2 = (bf16[1,128,576]{1,2,0:T(8,128)(2,1)S(1)}, bf16[1,128,576]{1,2,0:T(8,128)(2,1)}, u32[]{:S(2)}) copy-start(bf16[1,128,576]{1,2,0:T(8,128)(2,1)} %param.9) | copy-start | bytes 442372
  186.1 32.6 %all-to-all-start.4 = ((bf16[16,2,7168]{2,1,0:T(2,128)(2,1)}), bf16[16,2,7168]{2,1,0:T(2,128)(2,1)S(1)}, u32[]{:S(2)}, u32[]{:S(2)}) async-start(bf16[16,2,7168]{2,1,0:T(2,128)(2,1)} %convolution_convert_fusion.1), calls=%async_computation.4 | async-start | bytes 917504 | tf_op jit(solution)/shard_map/all_to_all | solution.py:92
where the time goes:
time: 221 us
  waiting for transfers between devices  93.3 us (42%)
  blocking collectives  54.7 us (25%)
  starting transfers between devices  35.7 us (16%)
  matrix products  14.2 us (6%)
  local copies, waits for them, and re-layouts  13 us (6%)
  other arithmetic  8.29 us (4%)
    all_to_all x1, blocking collectives, per_device(): lax.all_to_all(outgoing, 'local', split_axis=0, concat_axis=0, tiled=True)  54.7 us
    all_to_all x1, waiting for transfers between devices, per_device(): lax.all_to_all(slice_out.reshape(incoming.shape), 'local', split_axis=0,...  43.9 us
    all_to_all x1, waiting for transfers between devices, per_device(): lax.all_to_all(pair_out.astype(jnp.bfloat16), 'node', split_axis=0, conca...  24.9 us
    all_to_all x1, starting transfers between devices, per_device(): lax.all_to_all(send_gates, 'node', split_axis=0, concat_axis=0, tiled=True)  18.9 us
    all_to_all x1, waiting for transfers between devices, per_device(): lax.all_to_all(send_rows, 'node', split_axis=0, concat_axis=0, tiled=True)  16.7 us
    all_to_all x1, waiting for transfers between devices, per_device(): lax.all_to_all(send_gates, 'node', split_axis=0, concat_axis=0, tiled=True)  7.81 us
    all_to_all x1, starting transfers between devices, per_device(): lax.all_to_all(slice_out.reshape(incoming.shape), 'local', split_axis=0,...  7.41 us
    all_to_all x1, starting transfers between devices, per_device(): lax.all_to_all(pair_out.astype(jnp.bfloat16), 'node', split_axis=0, conca...  5.2 us
  transfers between devices with their start and end apart: 4, of which 4 were waited for; matrix products, arithmetic and copies ran while one was open for 3% of the time, Pallas kernels for 0%

commit v1 on v0

v1 whole, which is shorter than its diff:
```python
import jax
import jax.numpy as jnp
from jax import lax
from jax.experimental import pallas as pl
from jax.experimental.pallas import tpu as pltpu
from jax.sharding import PartitionSpec as P

MESH = pl.DeviceIdType.MESH
BF16, F32 = jnp.bfloat16, jnp.float32

D = 7168
HEADS = 128
CTX = 320
WIDTH = 576
LATENT = 512
HID = 64
EXPERTS = 64
E_NODE = 4
NZ, NX, NY, NC = 16, 4, 8, 2
PEERS = NX * NC
PIECE = 512
PIECES = D // PIECE
HALF = PIECES // 2
HALF_D = D // 2
ROWS = 16
GROUPS = ((0, 4), (4, 7))
SCALE = 192.0**-0.5


def iota(shape, dim):
    return lax.broadcasted_iota(jnp.int32, shape, dim)


def onehot(condition):
    return jnp.where(condition, 1.0, 0.0).astype(BF16)


def dot(a, b, dims=((1,), (0,))):
    return lax.dot_general(a, b, (dims, ((), ())), preferred_element_type=F32)


NT = ((1,), (1,))


def kernel(
    length_ref, block_ref, q_hbm, cache_hbm, gate_hbm, up_hbm, down_hbm,
    context_ref, out_ref,
    q_buf, cache_buf, score_buf, prob_buf, gu_buf, down_buf,
    z_buf, place_buf, x_send, x_recv, y_buf, pre_buf, pre_recv, part_buf,
    rs_send, rs_recv, b_send, b_recv, c_buf, c_recv, r_send, r_recv,
    in_sem, w_send_sem, w_recv_sem, z1_send, z1_recv, z2_send, z2_recv,
    x_ssem, x_rsem, y_ssem, y_rsem, p_ssem, p_rsem,
    s_ssem, s_rsem, b_ssem, b_rsem, c_ssem, c_rsem, r_ssem, r_rsem,
):
    g = lax.axis_index("node")
    l = lax.axis_index("local")
    x, y, c = l // 16, (l % 16) // 2, l % 2
    a, b = g // 4, g % 4
    me = x * NC + c
    other = 1 - c

    def at_z(step):
        return (lax.rem(g + step + NZ, NZ), l)

    def at_y(step):
        return (g, x * 16 + lax.rem(y + step + NY, NY) * 2 + c)

    def peer(n):
        return (g, (n // NC) * 16 + y * 2 + n % NC)

    twin = (g, l + 1 - 2 * c)

    def remote(src, dst, ssem, rsem, device):
        return pltpu.make_async_remote_copy(
            src_ref=src, dst_ref=dst, send_sem=ssem, recv_sem=rsem,
            device_id=device, device_id_type=MESH,
        )

    mine = pl.ds(pl.multiple_of(c * HALF_D, 128), HALF_D)
    theirs = pl.ds(pl.multiple_of(other * HALF_D, 128), HALF_D)
    own_copies = [
        pltpu.make_async_copy(q_hbm.at[0], q_buf, in_sem.at[0]),
        pltpu.make_async_copy(cache_hbm.at[0], cache_buf, in_sem.at[1]),
        pltpu.make_async_copy(gate_hbm.at[0, :, mine], gu_buf.at[c], in_sem.at[2]),
        pltpu.make_async_copy(up_hbm.at[0, :, mine], gu_buf.at[2 + c], in_sem.at[3]),
        pltpu.make_async_copy(down_hbm.at[0, :, mine], down_buf.at[c], in_sem.at[4]),
    ]
    for copy in own_copies:
        copy.start()
    sends = []

    barrier = pltpu.get_barrier_semaphore()
    z_steps = (1, -1, 2, -2, 4, 8, 12)
    partners = [at_z(s) for s in z_steps]
    partners += [peer(lax.rem(me + o, PEERS)) for o in range(1, PEERS)]
    partners += [at_y(1), at_y(-1)]
    for device in partners:
        pl.semaphore_signal(barrier, inc=1, device_id=device, device_id_type=MESH)
    z_buf[b, a] = block_ref[...]
    pl.semaphore_wait(barrier, len(partners))

    for o in range(1, 4):
        copy = remote(z_buf.at[b, a], z_buf.at[b, a], z1_send.at[o - 1], z1_recv.at[o - 1], at_z(4 * o))
        copy.start()
        sends.append(copy)
    for k, (hbm, buf, slot) in enumerate(
        ((gate_hbm, gu_buf, c), (up_hbm, gu_buf, 2 + c), (down_hbm, down_buf, c))
    ):
        copy = remote(hbm.at[0, :, theirs], buf.at[slot], w_send_sem.at[k], w_recv_sem.at[k], twin)
        copy.start()
        sends.append(copy)

    own_copies[0].wait()
    own_copies[1].wait()
    score_buf[...] = dot(q_buf[...], cache_buf[...], NT) * SCALE

    for o in range(1, 4):
        slot = z_buf.at[b, lax.rem(a - o + 4, 4)]
        remote(slot, slot, z1_send.at[o - 1], z1_recv.at[o - 1], at_z(4 * o)).wait_recv()
    far = 4 * (g % 2) - 2
    for k, step in enumerate((1, -1, far)):
        copy = remote(z_buf.at[b], z_buf.at[b], z2_send.at[k], z2_recv.at[k], at_z(step))
        copy.start()
        sends.append(copy)

    visible = iota((HEADS, CTX), 1) < length_ref[0]
    scores = jnp.where(visible, score_buf[...], -1e30)
    highest = jnp.max(scores, axis=1, keepdims=True)
    weights = jnp.where(visible, jnp.exp(scores - highest), 0.0)
    prob_buf[...] = (weights / jnp.sum(weights, axis=1, keepdims=True)).astype(BF16)

    col_x = iota((128, 256), 0) // 32
    col_h = iota((128, 256), 0) // 16 % 2
    col_k = iota((128, 256), 0) // 8 % 2
    col_j = iota((128, 256), 0) % 8
    row_j = iota((128, 256), 1) % 16
    expert_pick = onehot(iota((128, 128), 1) == E_NODE * g + iota((128, 128), 0) // 32)
    from_slot = iota((256, 256), 0) // 16
    from_j = iota((256, 256), 0) % 16
    to_slot = iota((256, 256), 1) // 16
    spread = onehot((from_slot == to_slot) & (from_j == PIECES))
    before = onehot((from_slot < to_slot) & (from_j == PIECES))
    right_piece = (row_j == HALF * col_h + col_j) & (col_j < HALF)

    for k, residue in enumerate((b + 3, b + 1, b + 2)):
        slot = z_buf.at[lax.rem(residue, 4)]
        remote(slot, slot, z2_send.at[k], z2_recv.at[k], at_z(1)).wait_recv()

    gathered = z_buf[...].reshape(256, PIECE)
    found = dot(expert_pick, gathered[:, :128], NT)
    found = jnp.where(row_j == PIECES, found, 0.0)
    taken = onehot(found > 0)
    slot_gate = dot(found.astype(BF16), spread)
    standing = dot(taken, before)
    chosen = (slot_gate > 0) & (standing == col_k.astype(F32)) & right_piece
    place = onehot(chosen)
    place_buf[...] = jnp.where(chosen, slot_gate, 0.0)
    x_send[...] = dot(place, gathered).astype(BF16).reshape(PEERS, 16, PIECE)
    for o in range(1, PEERS):
        to = lax.rem(me + o, PEERS)
        copy = remote(x_send.at[to], x_recv.at[me], x_ssem.at[o - 1], x_rsem.at[o - 1], peer(to))
        copy.start()
        sends.append(copy)
    x_recv[me] = x_send[me]

    context_ref[...] = dot(prob_buf[...], cache_buf[:, :LATENT]).astype(BF16)

    order_row = iota((HALF * ROWS, 128), 0)
    order_col = iota((HALF * ROWS, 128), 1)
    order = onehot(
        (order_row // 16 == order_col % 8)
        & (order_row % 16 // 2 == order_col // 16)
        & (order_row % 2 == order_col // 8 % 2)
    )
    for o in range(1, PEERS):
        slot = x_recv.at[lax.rem(me - o + PEERS, PEERS)]
        remote(slot, slot, x_ssem.at[o - 1], x_rsem.at[o - 1], peer(lax.rem(me + o, PEERS))).wait_recv()
    y_buf[0] = dot(order, x_recv[...].reshape(128, PIECE)).astype(BF16).reshape(HALF, ROWS, PIECE)

    def place_of(way, s):
        return 7 if s == 4 else 0 if s == 0 else 2 * s - 1 + way

    def gather(way, s, part):
        first, last = GROUPS[part]
        pieces = pl.ds(first, last - first)
        return remote(
            y_buf.at[place_of(way, s - 1), pieces], y_buf.at[place_of(way, s), pieces],
            y_ssem.at[way, s - 1, part], y_rsem.at[way, s - 1, part], at_y(1 - 2 * way),
        )

    def gather_wait(way, s, part):
        first, last = GROUPS[part]
        slot = y_buf.at[place_of(way, s), pl.ds(first, last - first)]
        remote(slot, slot, y_ssem.at[way, s - 1, part], y_rsem.at[way, s - 1, part], at_y(1 - 2 * way)).wait_recv()

    def project(first, last):
        rows = (last - first) * ROWS
        total = jnp.zeros((rows, 4 * HID), F32)
        for j in range(HALF):
            total += dot(
                y_buf[first:last, j].reshape(rows, PIECE),
                gu_buf[:, :, j * PIECE : (j + 1) * PIECE].reshape(4 * HID, PIECE),
                NT,
            )
        pre_buf[first * ROWS : last * ROWS, :] = total

    def exchange(k, first, last):
        rows = pl.ds(first * ROWS, (last - first) * ROWS)
        copy = remote(pre_buf.at[rows], pre_recv.at[rows], p_ssem.at[k], p_rsem.at[k], twin)
        copy.start()
        return copy

    def steps_of(s):
        return [(way, part) for part in range(2) for way in range(2) if s < 4 or part == way]

    for way, part in steps_of(1):
        copy = gather(way, 1, part)
        copy.start()
        sends.append(copy)
    for s in range(1, 4):
        for way, part in [(w, p) for p in range(2) for w in range(2)]:
            gather_wait(way, s, part)
            if (way, part) in steps_of(s + 1):
                copy = gather(way, s + 1, part)
                copy.start()
                sends.append(copy)
        if s == 1:
            for copy in own_copies[2:]:
                copy.wait()
            for k, (buf, slot) in enumerate(((gu_buf, other), (gu_buf, 2 + other), (down_buf, other))):
                ref = buf.at[slot]
                remote(ref, ref, w_send_sem.at[k], w_recv_sem.at[k], twin).wait_recv()
        if s == 2:
            project(0, 3)
        if s == 3:
            project(3, 7)
            exchanges = [exchange(0, 0, 7)]
    for way, part in steps_of(4):
        gather_wait(way, 4, part)
    project(7, 8)
    exchanges.append(exchange(1, 7, 8))
    for copy in exchanges:
        copy.wait_recv()
    sends += exchanges
    both = pre_buf[...] + pre_recv[...]
    gate_pre, up_pre = both[:, : 2 * HID], both[:, 2 * HID :]
    hidden = (gate_pre * jax.nn.sigmoid(gate_pre) * up_pre).astype(BF16)

    def down(part):
        for j in range(*GROUPS[part]):
            part_buf[:, j] = dot(
                hidden, down_buf[:, :, j * PIECE : (j + 1) * PIECE].reshape(2 * HID, PIECE)
            ).reshape(NY, ROWS, PIECE)

    def reduce_copy(way, s, part):
        first, last = GROUPS[part]
        pieces = pl.ds(first, last - first)
        return remote(
            rs_send.at[way, s - 1, pieces], rs_recv.at[way, s - 1, pieces],
            s_ssem.at[way, s - 1, part], s_rsem.at[way, s - 1, part], at_y(1 - 2 * way),
        )

    def reduce_send(way, s, part, received):
        first, last = GROUPS[part]
        total = part_buf[place_of(1 - way, 5 - s), first:last]
        if received:
            total = total + rs_recv[way, s - 2, first:last].astype(F32)
        rs_send[way, s - 1, first:last] = total.astype(BF16)
        copy = reduce_copy(way, s, part)
        copy.start()
        sends.append(copy)

    down(0)
    reduce_send(0, 1, 0, False)
    reduce_send(1, 2, 0, False)
    down(1)
    reduce_send(1, 1, 1, False)
    reduce_send(0, 2, 1, False)
    for s in range(2, 5):
        for part in range(2):
            for way in range(2):
                if s == 2 and part != way:
                    continue
                reduce_copy(way, s - 1, part).wait_recv()
                reduce_send(way, s, part, True)
    for part in range(2):
        first, last = GROUPS[part]
        for way in range(2):
            reduce_copy(way, 4, part).wait_recv()
            part_buf[0, first:last] += rs_recv[way, 3, first:last].astype(F32)

    back_row = iota((128, HALF * ROWS), 0)
    back_col = iota((128, HALF * ROWS), 1)
    back = onehot(
        (back_col // 16 == back_row % 8)
        & (back_col % 16 // 2 == back_row // 16)
        & (back_col % 2 == back_row // 8 % 2)
    )
    sums = part_buf[0].astype(BF16).reshape(HALF * ROWS, PIECE)
    b_send[...] = dot(back, sums).astype(BF16).reshape(PEERS, 16, PIECE)
    for o in range(1, PEERS):
        to = lax.rem(me + o, PEERS)
        copy = remote(b_send.at[to], b_recv.at[me], b_ssem.at[o - 1], b_rsem.at[o - 1], peer(to))
        copy.start()
        sends.append(copy)
    b_recv[me] = b_send[me]
    weigh = place_buf[...].T.astype(BF16)
    for o in range(1, PEERS):
        slot = b_recv.at[lax.rem(me - o + PEERS, PEERS)]
        remote(slot, slot, b_ssem.at[o - 1], b_rsem.at[o - 1], peer(lax.rem(me + o, PEERS))).wait_recv()

    c_buf[...] = dot(weigh, b_recv[...].reshape(128, PIECE)).astype(BF16).reshape(4, 4, 16, PIECE)
    for k, (step, residue) in enumerate(((1, b + 1), (-1, b + 3), (far, b + 2))):
        copy = remote(c_buf.at[lax.rem(residue, 4)], c_recv.at[k], c_ssem.at[k], c_rsem.at[k], at_z(step))
        copy.start()
        sends.append(copy)
    for k in range(3):
        remote(c_recv.at[k], c_recv.at[k], c_ssem.at[k], c_rsem.at[k], at_z(1)).wait_recv()
    near = c_buf[b].astype(F32)
    for k in range(3):
        near = near + c_recv[k].astype(F32)
    r_send[...] = near.astype(BF16)
    for o in range(1, 4):
        copy = remote(
            r_send.at[lax.rem(a + o, 4)], r_recv.at[o - 1], r_ssem.at[o - 1], r_rsem.at[o - 1], at_z(4 * o)
        )
        copy.start()
        sends.append(copy)
    total = r_send[a].astype(F32)
    for o in range(1, 4):
        remote(r_recv.at[o - 1], r_recv.at[o - 1], r_ssem.at[o - 1], r_rsem.at[o - 1], at_z(4 * o)).wait_recv()
        total = total + r_recv[o - 1].astype(F32)
    out_ref[...] = total.astype(BF16)
    for copy in sends:
        copy.wait_send()


def per_device(queries, latent_cache, lengths, moe_rows, expert_ids, route_gates, w_gate, w_up, w_down):
    picks = expert_ids[0][:, None] == jnp.arange(PIECE)[None, :]
    gates = jnp.sum(jnp.where(picks, route_gates[0][:, None].astype(F32), 0.0), axis=0)
    tail = jnp.stack([gates, jnp.zeros_like(gates)]).astype(BF16)
    block = jnp.concatenate([moe_rows.reshape(PIECES, PIECE), tail])

    any_spec = pl.BlockSpec(memory_space=pl.ANY)
    vmem_spec = pl.BlockSpec(memory_space=pltpu.VMEM)
    dma = pltpu.SemaphoreType.DMA
    context, out = pl.pallas_call(
        kernel,
        out_shape=(
            jax.ShapeDtypeStruct((HEADS, LATENT), BF16),
            jax.ShapeDtypeStruct((16, PIECE), BF16),
        ),
        in_specs=[pl.BlockSpec(memory_space=pltpu.SMEM), vmem_spec] + [any_spec] * 5,
        out_specs=(vmem_spec, vmem_spec),
        scratch_shapes=[
            pltpu.VMEM((HEADS, WIDTH), BF16),
            pltpu.VMEM((CTX, WIDTH), BF16),
            pltpu.VMEM((HEADS, CTX), F32),
            pltpu.VMEM((HEADS, CTX), BF16),
            pltpu.VMEM((4, HID, HALF_D), BF16),
            pltpu.VMEM((2, HID, HALF_D), BF16),
            pltpu.VMEM((4, 4, 16, PIECE), BF16),
            pltpu.VMEM((128, 256), F32),
            pltpu.VMEM((PEERS, 16, PIECE), BF16),
            pltpu.VMEM((PEERS, 16, PIECE), BF16),
            pltpu.VMEM((NY, HALF, ROWS, PIECE), BF16),
            pltpu.VMEM((128, 4 * HID), F32),
            pltpu.VMEM((128, 4 * HID), F32),
            pltpu.VMEM((NY, HALF, ROWS, PIECE), F32),
            pltpu.VMEM((2, 4, HALF, ROWS, PIECE), BF16),
            pltpu.VMEM((2, 4, HALF, ROWS, PIECE), BF16),
            pltpu.VMEM((PEERS, 16, PIECE), BF16),
            pltpu.VMEM((PEERS, 16, PIECE), BF16),
            pltpu.VMEM((4, 4, 16, PIECE), BF16),
            pltpu.VMEM((3, 4, 16, PIECE), BF16),
            pltpu.VMEM((4, 16, PIECE), BF16),
            pltpu.VMEM((3, 16, PIECE), BF16),
            dma((5,)), dma((3,)), dma((3,)),
            dma((3,)), dma((3,)), dma((3,)), dma((3,)),
            dma((7,)), dma((7,)),
            dma((2, 4, 2)), dma((2, 4, 2)),
            dma((2,)), dma((2,)),
            dma((2, 4, 2)), dma((2, 4, 2)),
            dma((7,)), dma((7,)),
            dma((3,)), dma((3,)), dma((3,)), dma((3,)),
        ],
        compiler_params=pltpu.CompilerParams(
            collective_id=0, has_side_effects=True, vmem_limit_bytes=40 * 1024 * 1024
        ),
        cost_estimate=pl.CostEstimate(flops=1_000_000_000, bytes_accessed=4_000_000, transcendentals=50_000),
    )(lengths, block, queries, latent_cache, w_gate, w_up, w_down)
    return context[None], out[:PIECES].reshape(1, D)


def solution(mesh):
    rows = P(("node", "local"), None)
    wide = P(("node", "local"), None, None)
    return jax.shard_map(
        per_device,
        mesh=mesh,
        in_specs=(wide, wide, P(("node", "local")), rows, rows, rows, wide, wide, wide),
        out_specs=(wide, rows),
        check_vma=False,
    )
```

time: 221 us -> 102 us (0.46)
  the two profiles are of different devices: /device:TPU:14 before, /device:TPU:16 now
where the time goes in v1:
time: 102 us; the launch traced here: 101 us
  Pallas kernels  91.9 us (90%)
  local copies, waits for them, and re-layouts  5.92 us (6%)
  other arithmetic  2.24 us (2%)
  between operations  1.39 us (1%)
    pallas_call x1, Pallas kernels, per_device(): pl.pallas_call(kernel, out_shape=(jax.ShapeDtypeStruct((HEADS, LATENT), B...  91.9 us
    unnamed x12, local copies, waits for them, and re-layouts  5.89 us

profile of v1, /device:TPU:16, one launch (start us, length us, event | category | flops | bytes accessed | tf_op | source)
XLA Modules:
  0.0 101.4 jit_solution(6480608915019776231)
XLA Ops:
  0.6 0.0 copy-start.3
  1.3 0.7 bitcast_convert_fusion
  2.0 0.7 select_reduce_fusion
  2.7 0.8 reduce
  3.6 1.1 %copy.12.q_hbm = bf16[1,128,576]{2,1,0:T(8,128)(2,1)S(1)} copy(bf16[1,128,576]{1,2,0:T(8,128)(2,1)} %param.9) | data formatting | bytes 294912 | tf_op args[0]
  4.7 0.0 copy-done.3
  4.7 0.0 copy-start
  4.7 1.2 %copy-done = bf16[1,64,7168]{2,1,0:T(8,128)(2,1)S(1)} copy-done((bf16[1,64,7168]{2,1,0:T(8,128)(2,1)S(1)}, bf16[1,64,7168]{2,1,0:T(8,128)(2,1)}, u32[]{:S(2)}) %copy-start) | copy-done | bytes 917528
  5.9 0.0 copy-start.1
  5.9 1.2 %copy-done.1 = bf16[1,64,7168]{2,1,0:T(8,128)(2,1)S(1)} copy-done((bf16[1,64,7168]{2,1,0:T(8,128)(2,1)S(1)}, bf16[1,64,7168]{2,1,0:T(8,128)(2,1)}, u32[]{:S(2)}) %copy-start.1) | copy-done | bytes 917528
  7.1 0.0 copy-start.2
  7.1 1.2 %copy-done.2 = bf16[1,64,7168]{2,1,0:T(8,128)(2,1)S(1)} copy-done((bf16[1,64,7168]{2,1,0:T(8,128)(2,1)S(1)}, bf16[1,64,7168]{2,1,0:T(8,128)(2,1)}, u32[]{:S(2)}) %copy-start.2) | copy-done | bytes 917528
  8.2 91.9 %shard_map.104 = (bf16[128,512]{1,0:T(8,128)(2,1)S(1)}, bf16[16,512]{1,0:T(8,128)(2,1)S(1)}) custom-call(s32[1]{0:T(128)S(6)} %copy.15.length_ref, bf16[16,512]{1,0:T(8,128)(2,1)S(1)} %fusion.1.block_ref, bf16[1,128,576]{2,1,0:T(8,128)(2,1)S(1)} %copy.12.q_hbm, bf16[1,320,576]{2,1,0:T(8,128)(2,1)S(1)} %copy-done.3, bf16[1,64,7168]{2,1,0:T(8,128)(2,1)S(1)} %copy-done, ...), custom_call_target="tpu_custom_call" | custom-call | flops 1000000000 | bytes 4000000 | tf_op jit(solution)/shard_map/pallas_call | solution.py:347
  100.1 0.6 copy.13
  100.8 0.7 copy.16
  (4 shorter events, 0.0 us)
Async XLA Ops:
  0.6 4.1 %copy-start.3 = (bf16[1,320,576]{2,1,0:T(8,128)(2,1)S(1)}, bf16[1,320,576]{2,1,0:T(8,128)(2,1)}, u32[]{:S(2)}) copy-start(bf16[1,320,576]{2,1,0:T(8,128)(2,1)} %cache_hbm.1) | copy-start | bytes 1105924
  4.7 1.2 %copy-start = (bf16[1,64,7168]{2,1,0:T(8,128)(2,1)S(1)}, bf16[1,64,7168]{2,1,0:T(8,128)(2,1)}, u32[]{:S(2)}) copy-start(bf16[1,64,7168]{2,1,0:T(8,128)(2,1)} %gate_hbm.1) | copy-start | bytes 2752516
  5.9 1.2 %copy-start.1 = (bf16[1,64,7168]{2,1,0:T(8,128)(2,1)S(1)}, bf16[1,64,7168]{2,1,0:T(8,128)(2,1)}, u32[]{:S(2)}) copy-start(bf16[1,64,7168]{2,1,0:T(8,128)(2,1)} %up_hbm.1) | copy-start | bytes 2752516
  7.1 1.2 %copy-start.2 = (bf16[1,64,7168]{2,1,0:T(8,128)(2,1)S(1)}, bf16[1,64,7168]{2,1,0:T(8,128)(2,1)}, u32[]{:S(2)}) copy-start(bf16[1,64,7168]{2,1,0:T(8,128)(2,1)} %down_hbm.1) | copy-start | bytes 2752516

commit v2 on v1

v2 whole, which is shorter than its diff:
```python
import jax
import jax.numpy as jnp
from jax import lax
from jax.experimental import pallas as pl
from jax.experimental.pallas import tpu as pltpu
from jax.sharding import PartitionSpec as P

MESH = pl.DeviceIdType.MESH
BF16, F32 = jnp.bfloat16, jnp.float32

D = 7168
HEADS = 128
CTX = 320
WIDTH = 576
LATENT = 512
HID = 64
EXPERTS = 64
E_NODE = 4
NZ, NX, NY, NC = 16, 4, 8, 2
PEERS = NX * NC
PIECE = 512
PIECES = D // PIECE
HALF = PIECES // 2
HALF_D = D // 2
ROWS = 16
GROUPS = ((0, 4), (4, 7))
SCALE = 192.0**-0.5


def iota(shape, dim):
    return lax.broadcasted_iota(jnp.int32, shape, dim)


def onehot(condition):
    return jnp.where(condition, 1.0, 0.0).astype(BF16)


def dot(a, b, dims=((1,), (0,))):
    return lax.dot_general(a, b, (dims, ((), ())), preferred_element_type=F32)


NT = ((1,), (1,))
TN = ((0,), (0,))


def kernel(
    length_ref, row_ref, id_ref, gate_ref, q_hbm, cache_hbm, gate_hbm, up_hbm, down_hbm,
    context_ref, out_ref,
    q_buf, cache_buf, score_buf, prob_buf, gu_buf, down_buf,
    z_buf, place_buf, x_send, x_recv, y_buf, pre_mid, mid_recv, pre_end, end_recv, part_buf,
    rs_send, rs_recv, b_send, b_recv, c_buf, c_recv, r_send, r_recv, filler,
    in_sem, w_send_sem, w_recv_sem, z1_send, z1_recv, z2_send, z2_recv,
    x_ssem, x_rsem, y_ssem, y_rsem, p_ssem, p_rsem,
    s_ssem, s_rsem, b_ssem, b_rsem, c_ssem, c_rsem, r_ssem, r_rsem,
):
    g = lax.axis_index("node")
    l = lax.axis_index("local")
    x, y, c = l // 16, (l % 16) // 2, l % 2
    a, b = g // 4, g % 4
    me = x * NC + c
    other = 1 - c

    def at_z(step):
        return (lax.rem(g + step + NZ, NZ), l)

    def at_y(step):
        return (g, x * 16 + lax.rem(y + step + NY, NY) * 2 + c)

    def peer(n):
        return (g, (n // NC) * 16 + y * 2 + n % NC)

    twin = (g, l + 1 - 2 * c)

    def remote(src, dst, ssem, rsem, device):
        return pltpu.make_async_remote_copy(
            src_ref=src, dst_ref=dst, send_sem=ssem, recv_sem=rsem,
            device_id=device, device_id_type=MESH,
        )

    mine = pl.ds(pl.multiple_of(c * HALF_D, 128), HALF_D)
    theirs = pl.ds(pl.multiple_of(other * HALF_D, 128), HALF_D)
    own_copies = [
        pltpu.make_async_copy(q_hbm.at[0], q_buf, in_sem.at[0]),
        pltpu.make_async_copy(cache_hbm.at[0], cache_buf, in_sem.at[1]),
        pltpu.make_async_copy(gate_hbm.at[0, :, mine], gu_buf.at[c], in_sem.at[2]),
        pltpu.make_async_copy(up_hbm.at[0, :, mine], gu_buf.at[2 + c], in_sem.at[3]),
        pltpu.make_async_copy(down_hbm.at[0, :, mine], down_buf.at[c], in_sem.at[4]),
    ]
    for copy in own_copies:
        copy.start()
    sends = []

    barrier = pltpu.get_barrier_semaphore()
    z_steps = (1, -1, 2, -2, 4, 8, 12)
    partners = [at_z(s) for s in z_steps]
    partners += [peer(lax.rem(me + o, PEERS)) for o in range(1, PEERS)]
    partners += [at_y(1), at_y(-1)]
    for device in partners:
        pl.semaphore_signal(barrier, inc=1, device_id=device, device_id_type=MESH)
    lane = iota((1, PIECE), 1)
    gates = jnp.zeros((1, PIECE), F32)
    for k in range(8):
        gates = gates + jnp.where(lane == id_ref[:, k : k + 1], gate_ref[:, k : k + 1].astype(F32), 0.0)
    pieces = [row_ref[:, j * PIECE : (j + 1) * PIECE].astype(F32) for j in range(PIECES)]
    z_buf[b, a] = jnp.concatenate(pieces + [gates, jnp.zeros((1, PIECE), F32)], axis=0).astype(BF16)
    pl.semaphore_wait(barrier, len(partners))

    for o in (2, 1, 3):
        copy = remote(z_buf.at[b, a], z_buf.at[b, a], z1_send.at[o - 1], z1_recv.at[o - 1], at_z(4 * o))
        copy.start()
        sends.append(copy)
    far = 4 * (g % 2) - 2
    near_steps = (1, -1, far)

    def hand_on(o):
        slot = z_buf.at[b, lax.rem(a - o + 4, 4)]
        for k, step in enumerate(near_steps):
            copy = remote(slot, slot, z2_send.at[k, o], z2_recv.at[k, o], at_z(step))
            copy.start()
            sends.append(copy)

    hand_on(0)
    for k, (hbm, buf, slot) in enumerate(
        ((gate_hbm, gu_buf, c), (up_hbm, gu_buf, 2 + c), (down_hbm, down_buf, c))
    ):
        copy = remote(hbm.at[0, :, theirs], buf.at[slot], w_send_sem.at[k], w_recv_sem.at[k], twin)
        copy.start()
        sends.append(copy)

    own_copies[0].wait()
    own_copies[1].wait()
    score_buf[...] = dot(cache_buf[...], q_buf[...]) * SCALE
    visible = iota((CTX, HEADS), 0) < length_ref[0]
    scores = jnp.where(visible, score_buf[...], -1e30)
    highest = jnp.max(scores, axis=0, keepdims=True)
    weights = jnp.where(visible, jnp.exp(scores - highest), 0.0)
    prob_buf[...] = (weights / jnp.sum(weights, axis=0, keepdims=True)).astype(BF16)

    column = iota((128, 256), 0)
    col_j = column & 7
    row_j = iota((128, 256), 1) & 15
    expert_pick = onehot(iota((128, 128), 1) == E_NODE * g + (iota((128, 128), 0) >> 5))
    from_row = iota((256, 256), 0)
    from_slot, from_tail = from_row >> 4, (from_row & 15) == PIECES
    to_slot = iota((256, 256), 1) >> 4
    spread = onehot((from_slot == to_slot) & from_tail)
    before = onehot((from_slot < to_slot) & from_tail)
    right_piece = (row_j == HALF * (column >> 4 & 1) + col_j) & (col_j < HALF)
    wanted_standing = (column >> 3 & 1).astype(F32)

    order_row = iota((HALF * ROWS, 128), 0)
    order_col = iota((HALF * ROWS, 128), 1)
    order = onehot(
        (order_row >> 4 == (order_col & 7))
        & ((order_row & 15) >> 1 == order_col >> 4)
        & ((order_row & 1) == (order_col >> 3 & 1))
    )

    pre_mid[...] = jnp.zeros_like(pre_mid)

    for o in (1, 3, 2):
        slot = z_buf.at[b, lax.rem(a - o + 4, 4)]
        remote(slot, slot, z1_send.at[o - 1], z1_recv.at[o - 1], at_z(4 * o)).wait_recv()
        hand_on(o)

    context_ref[...] = dot(prob_buf[...], cache_buf[:, :LATENT], TN).astype(BF16)

    for o in (0, 1, 3, 2):
        for k, step in enumerate(near_steps):
            plane = lax.rem(g - step + NZ, NZ)
            slot = z_buf.at[plane % 4, lax.rem(plane // 4 - o + 4, 4)]
            remote(slot, slot, z2_send.at[k, o], z2_recv.at[k, o], at_z(step)).wait_recv()
    gathered = z_buf[...].reshape(256, PIECE)
    found = dot(expert_pick, gathered[:, :128], NT)
    found = jnp.where(row_j == PIECES, found, 0.0)
    taken = onehot(found > 0)
    slot_gate = dot(found.astype(BF16), spread)
    standing = dot(taken, before)
    chosen = (slot_gate > 0) & (standing == wanted_standing) & right_piece
    place = onehot(chosen)
    place_buf[...] = jnp.where(chosen, slot_gate, 0.0)
    x_send[...] = dot(place, gathered).astype(BF16).reshape(PEERS, 16, PIECE)
    for o in range(1, PEERS):
        to = lax.rem(me + o, PEERS)
        copy = remote(x_send.at[to], x_recv.at[me], x_ssem.at[o - 1], x_rsem.at[o - 1], peer(to))
        copy.start()
        sends.append(copy)
    x_recv[me] = x_send[me]

    for o in range(1, PEERS):
        slot = x_recv.at[lax.rem(me - o + PEERS, PEERS)]
        remote(slot, slot, x_ssem.at[o - 1], x_rsem.at[o - 1], peer(lax.rem(me + o, PEERS))).wait_recv()
    y_buf[0] = dot(order, x_recv[...].reshape(128, PIECE)).astype(BF16).reshape(HALF, ROWS, PIECE)

    def place_of(way, s):
        return 7 if s == 4 else 0 if s == 0 else 2 * s - 1 + way

    def gather(way, s, j):
        return remote(
            y_buf.at[place_of(way, s - 1), j], y_buf.at[place_of(way, s), j],
            y_ssem.at[way, s - 1, j], y_rsem.at[way, s - 1, j], at_y(1 - 2 * way),
        )

    def gather_wait(way, s, j):
        slot = y_buf.at[place_of(way, s), j]
        remote(slot, slot, y_ssem.at[way, s - 1, j], y_rsem.at[way, s - 1, j], at_y(1 - 2 * way)).wait_recv()

    def weight_piece(j):
        return gu_buf[:, :, j * PIECE : (j + 1) * PIECE].reshape(4 * HID, PIECE)

    last_way = [0] * GROUPS[0][1] + [1] * (HALF - GROUPS[0][1])

    def steps_of(s):
        return [(way, j) for j in range(HALF) for way in range(2) if s < 4 or last_way[j] == way]

    for way, j in steps_of(1):
        copy = gather(way, 1, j)
        copy.start()
        sends.append(copy)
    for s in range(1, 4):
        for way, j in steps_of(s):
            gather_wait(way, s, j)
            if (way, j) in steps_of(s + 1):
                copy = gather(way, s + 1, j)
                copy.start()
                sends.append(copy)
        if s == 1:
            for copy in own_copies[2:]:
                copy.wait()
            for k, (buf, slot) in enumerate(((gu_buf, other), (gu_buf, 2 + other), (down_buf, other))):
                ref = buf.at[slot]
                remote(ref, ref, w_send_sem.at[k], w_recv_sem.at[k], twin).wait_recv()
        if s == 3:
            rows = 7 * ROWS
            total = jnp.zeros((4 * HID, rows), F32)
            for j in range(HALF):
                total += dot(weight_piece(j), y_buf[:7, j].reshape(rows, PIECE), NT)
            pre_mid[:, :rows] = total
            mid = remote(pre_mid, mid_recv, p_ssem.at[0], p_rsem.at[0], twin)
            mid.start()
            sends.append(mid)
    for way, j in steps_of(4):
        gather_wait(way, 4, j)
    total = jnp.zeros((ROWS, 4 * HID), F32)
    for j in range(HALF):
        total += dot(y_buf[7, j], weight_piece(j), NT)
    pre_end[...] = total
    end = remote(pre_end, end_recv, p_ssem.at[1], p_rsem.at[1], twin)
    end.start()
    sends.append(end)

    def down(hidden, j):
        return dot(hidden, down_buf[:, :, j * PIECE : (j + 1) * PIECE].reshape(2 * HID, PIECE))

    def reduce_copy(way, s, j):
        return remote(
            rs_send.at[way, s - 1, j], rs_recv.at[way, s - 1, j],
            s_ssem.at[way, s - 1, j], s_rsem.at[way, s - 1, j], at_y(1 - 2 * way),
        )

    def reduce_send(way, s, j, received):
        total = part_buf[place_of(1 - way, 5 - s), j]
        if received:
            total = total + rs_recv[way, s - 2, j].astype(F32)
        rs_send[way, s - 1, j] = total.astype(BF16)
        copy = reduce_copy(way, s, j)
        copy.start()
        sends.append(copy)

    mid.wait_recv()
    both = pre_mid[...] + mid_recv[...]
    gate_pre, up_pre = both[: 2 * HID], both[2 * HID :]
    hidden = (gate_pre * jax.nn.sigmoid(gate_pre) * up_pre).T[: 7 * ROWS].astype(BF16)
    turns = [j for pair in zip(range(4), (4, 5, 6, None)) for j in pair if j is not None]
    for j in turns:
        part_buf[:, j] = down(hidden, j).reshape(7, ROWS, PIECE)
        reduce_send(1 - last_way[j], 2, j, False)
    end.wait_recv()
    both = pre_end[...] + end_recv[...]
    gate_pre, up_pre = both[:, : 2 * HID], both[:, 2 * HID :]
    hidden = (gate_pre * jax.nn.sigmoid(gate_pre) * up_pre).astype(BF16)
    for j in turns:
        way = last_way[j]
        rs_send[way, 0, j] = down(hidden, j).astype(BF16)
        copy = reduce_copy(way, 1, j)
        copy.start()
        sends.append(copy)
    for j in turns:
        way = last_way[j]
        reduce_copy(way, 1, j).wait_recv()
        reduce_send(way, 2, j, True)
    early = [(1 - last_way[j], j) for j in turns] + [(last_way[j], j) for j in turns]
    for s in range(3, 5):
        for way, j in early:
            reduce_copy(way, s - 1, j).wait_recv()
            reduce_send(way, s, j, True)
    for way, j in early:
        reduce_copy(way, 4, j).wait_recv()
        part_buf[0, j] += rs_recv[way, 3, j].astype(F32)

    sums = part_buf[0].astype(BF16).reshape(HALF * ROWS, PIECE)
    b_send[...] = dot(order, sums, TN).astype(BF16).reshape(PEERS, 16, PIECE)
    for o in range(1, PEERS):
        to = lax.rem(me + o, PEERS)
        copy = remote(b_send.at[to], b_recv.at[me], b_ssem.at[o - 1], b_rsem.at[o - 1], peer(to))
        copy.start()
        sends.append(copy)
    b_recv[me] = b_send[me]
    weigh = place_buf[...].T.astype(BF16)
    for o in range(1, PEERS):
        slot = b_recv.at[lax.rem(me - o + PEERS, PEERS)]
        remote(slot, slot, b_ssem.at[o - 1], b_rsem.at[o - 1], peer(lax.rem(me + o, PEERS))).wait_recv()

    c_buf[...] = dot(weigh, b_recv[...].reshape(128, PIECE)).astype(BF16).reshape(4, 4, 16, PIECE)
    for o in (2, 1, 3, 0):
        for k, step in enumerate(near_steps):
            plane = lax.rem(g + step + NZ, NZ)
            copy = remote(
                c_buf.at[plane % 4, lax.rem(plane // 4 + o, 4)], c_recv.at[k, o],
                c_ssem.at[k, o], c_rsem.at[k, o], at_z(step),
            )
            copy.start()
            sends.append(copy)
    for o in (2, 1, 3, 0):
        total = c_buf[b, lax.rem(a + o, 4)].astype(F32)
        for k in range(3):
            remote(c_recv.at[k, o], c_recv.at[k, o], c_ssem.at[k, o], c_rsem.at[k, o], at_z(1)).wait_recv()
            total = total + c_recv[k, o].astype(F32)
        if o > 0:
            r_send[o - 1] = total.astype(BF16)
            copy = remote(r_send.at[o - 1], r_recv.at[o - 1], r_ssem.at[o - 1], r_rsem.at[o - 1], at_z(4 * o))
            copy.start()
            sends.append(copy)
    for o in (1, 3, 2):
        remote(r_recv.at[o - 1], r_recv.at[o - 1], r_ssem.at[o - 1], r_rsem.at[o - 1], at_z(4 * o)).wait_recv()
        total = total + r_recv[o - 1].astype(F32)
    for j in range(PIECES):
        out_ref[:, j * PIECE : (j + 1) * PIECE] = total[j : j + 1].astype(BF16)
    for copy in sends:
        copy.wait_send()


def per_device(queries, latent_cache, lengths, moe_rows, expert_ids, route_gates, w_gate, w_up, w_down):
    any_spec = pl.BlockSpec(memory_space=pl.ANY)
    vmem_spec = pl.BlockSpec(memory_space=pltpu.VMEM)
    dma = pltpu.SemaphoreType.DMA
    context, out = pl.pallas_call(
        kernel,
        out_shape=(
            jax.ShapeDtypeStruct((HEADS, LATENT), BF16),
            jax.ShapeDtypeStruct((1, D), BF16),
        ),
        in_specs=[pl.BlockSpec(memory_space=pltpu.SMEM)] + [vmem_spec] * 3 + [any_spec] * 5,
        out_specs=(vmem_spec, vmem_spec),
        scratch_shapes=[
            pltpu.VMEM((WIDTH, HEADS), BF16),
            pltpu.VMEM((CTX, WIDTH), BF16),
            pltpu.VMEM((CTX, HEADS), F32),
            pltpu.VMEM((CTX, HEADS), BF16),
            pltpu.VMEM((4, HID, HALF_D), BF16),
            pltpu.VMEM((2, HID, HALF_D), BF16),
            pltpu.VMEM((4, 4, 16, PIECE), BF16),
            pltpu.VMEM((128, 256), F32),
            pltpu.VMEM((PEERS, 16, PIECE), BF16),
            pltpu.VMEM((PEERS, 16, PIECE), BF16),
            pltpu.VMEM((NY, HALF, ROWS, PIECE), BF16),
            pltpu.VMEM((4 * HID, 128), F32),
            pltpu.VMEM((4 * HID, 128), F32),
            pltpu.VMEM((ROWS, 4 * HID), F32),
            pltpu.VMEM((ROWS, 4 * HID), F32),
            pltpu.VMEM((NY - 1, HALF, ROWS, PIECE), F32),
            pltpu.VMEM((2, 4, HALF, ROWS, PIECE), BF16),
            pltpu.VMEM((2, 4, HALF, ROWS, PIECE), BF16),
            pltpu.VMEM((PEERS, 16, PIECE), BF16),
            pltpu.VMEM((PEERS, 16, PIECE), BF16),
            pltpu.VMEM((4, 4, 16, PIECE), BF16),
            pltpu.VMEM((3, 4, 16, PIECE), BF16),
            pltpu.VMEM((3, 16, PIECE), BF16),
            pltpu.VMEM((3, 16, PIECE), BF16),
            pltpu.VMEM((2880, 8192), BF16),
            dma((5,)), dma((3,)), dma((3,)),
            dma((3,)), dma((3,)), dma((3, 4)), dma((3, 4)),
            dma((7,)), dma((7,)),
            dma((2, 4, 7)), dma((2, 4, 7)),
            dma((2,)), dma((2,)),
            dma((2, 4, 7)), dma((2, 4, 7)),
            dma((7,)), dma((7,)),
            dma((3, 4)), dma((3, 4)), dma((3,)), dma((3,)),
        ],
        compiler_params=pltpu.CompilerParams(
            collective_id=0, has_side_effects=True, vmem_limit_bytes=60 * 1024 * 1024
        ),
        cost_estimate=pl.CostEstimate(flops=1_000_000_000, bytes_accessed=4_000_000, transcendentals=50_000),
    )(lengths, moe_rows, expert_ids, route_gates, jnp.swapaxes(queries, 1, 2), latent_cache, w_gate, w_up, w_down)
    return context[None], out


def solution(mesh):
    rows = P(("node", "local"), None)
    wide = P(("node", "local"), None, None)
    return jax.shard_map(
        per_device,
        mesh=mesh,
        in_specs=(wide, wide, P(("node", "local")), rows, rows, rows, wide, wide, wide),
        out_specs=(wide, rows),
        check_vma=False,
    )
```

time: 102 us -> 92.8 us (0.910)
  the two profiles are of different devices: /device:TPU:16 before, /device:TPU:4 now
where the time goes in v2:
time: 92.8 us; the launch traced here: 92.6 us
  Pallas kernels  89.1 us (96%)
  local copies, waits for them, and re-layouts  2.19 us (2%)
  between operations  1.29 us (1%)
    pallas_call x1, Pallas kernels, per_device(): pl.pallas_call(kernel, out_shape=(jax.ShapeDtypeStruct((HEADS, LATENT), B...  89.1 us
    unnamed x4, local copies, waits for them, and re-layouts  2.19 us

profile of v2, /device:TPU:4, one launch (start us, length us, event | category | flops | bytes accessed | tf_op | source)
XLA Modules:
  0.0 92.6 jit_solution(3017608063904964865)
XLA Ops:
  1.3 89.1 %shard_map.104 = (bf16[128,512]{1,0:T(8,128)(2,1)}, bf16[1,7168]{1,0:T(2,128)(2,1)}) custom-call(s32[1]{0:T(128)S(6)} %copy.13.length_ref, bf16[1,7168]{1,0:T(2,128)(2,1)} %row_ref.1, s32[1,8]{1,0:T(1,128)} %id_ref.1, bf16[1,8]{1,0:T(2,128)(2,1)} %gate_ref.1, bf16[1,576,128]{2,1,0:T(8,128)(2,1)} %bitcast.3, bf16[1,320,576]{2,1,0:T(8,128)(2,1)} %cache_hbm.1, ...), custom_call_target="tpu_custom_call" | custom-call | flops 1000000000 | bytes 4000000 | tf_op jit(solution)/shard_map/pallas_call | solution.py:347
  90.4 0.0 copy-start
  90.4 1.6 %copy.14 = bf16[1,128,512]{2,1,0:T(8,128)(2,1)} copy(bf16[1,128,512]{2,1,0:T(8,128)(2,1)} %bitcast.2) | data formatting | bytes 262144
  92.0 0.0 copy-done
  92.0 0.6 copy.15
Async XLA Ops:
  90.4 1.6 %copy-start = (bf16[1,7168]{1,0:T(2,128)(2,1)S(1)}, bf16[1,7168]{1,0:T(2,128)(2,1)}, u32[]{:S(2)}) copy-start(bf16[1,7168]{1,0:T(2,128)(2,1)} %get-tuple-element.9) | copy-start | bytes 43012

commit v3 on v2

--- a/solution.py
+++ b/solution.py
@@ -20,6 +20,7 @@
 PEERS = NX * NC
 PIECE = 512
 PIECES = D // PIECE
+LANES = PIECE // 2
 HALF = PIECES // 2
 HALF_D = D // 2
 ROWS = 16
@@ -48,7 +49,7 @@
     context_ref, out_ref,
     q_buf, cache_buf, score_buf, prob_buf, gu_buf, down_buf,
     z_buf, place_buf, x_send, x_recv, y_buf, pre_mid, mid_recv, pre_end, end_recv, part_buf,
-    rs_send, rs_recv, b_send, b_recv, c_buf, c_recv, r_send, r_recv, filler,
+    rs_send, rs_recv, b_send, b_recv, c_buf, c_recv, r_send, r_recv,
     in_sem, w_send_sem, w_recv_sem, z1_send, z1_recv, z2_send, z2_recv,
     x_ssem, x_rsem, y_ssem, y_rsem, p_ssem, p_rsem,
     s_ssem, s_rsem, b_ssem, b_rsem, c_ssem, c_rsem, r_ssem, r_rsem,
@@ -102,39 +103,34 @@
     for k in range(8):
         gates = gates + jnp.where(lane == id_ref[:, k : k + 1], gate_ref[:, k : k + 1].astype(F32), 0.0)
     pieces = [row_ref[:, j * PIECE : (j + 1) * PIECE].astype(F32) for j in range(PIECES)]
-    z_buf[b, a] = jnp.concatenate(pieces + [gates, jnp.zeros((1, PIECE), F32)], axis=0).astype(BF16)
+    block = jnp.concatenate(pieces + [gates, jnp.zeros((1, PIECE), F32)], axis=0).astype(BF16)
+    for q in range(2):
+        z_buf[q, b, a] = block[:, q * LANES : (q + 1) * LANES]
     pl.semaphore_wait(barrier, len(partners))
 
-    for o in (2, 1, 3):
-        copy = remote(z_buf.at[b, a], z_buf.at[b, a], z1_send.at[o - 1], z1_recv.at[o - 1], at_z(4 * o))
-        copy.start()
-        sends.append(copy)
     far = 4 * (g % 2) - 2
     near_steps = (1, -1, far)
 
-    def hand_on(o):
-        slot = z_buf.at[b, lax.rem(a - o + 4, 4)]
+    def hand_on(q, o):
+        slot = z_buf.at[q, b, lax.rem(a - o + 4, 4)]
         for k, step in enumerate(near_steps):
-            copy = remote(slot, slot, z2_send.at[k, o], z2_recv.at[k, o], at_z(step))
-            copy.start()
-            sends.append(copy)
-
-    hand_on(0)
+            copy = remote(slot, slot, z2_send.at[q, k, o], z2_recv.at[q, k, o], at_z(step))
+            copy.start()
+            sends.append(copy)
+
+    for q in range(2):
+        slot = z_buf.at[q, b, a]
+        for o in (2, 1, 3):
+            copy = remote(slot, slot, z1_send.at[q, o - 1], z1_recv.at[q, o - 1], at_z(4 * o))
+            copy.start()
+            sends.append(copy)
+        hand_on(q, 0)
     for k, (hbm, buf, slot) in enumerate(
         ((gate_hbm, gu_buf, c), (up_hbm, gu_buf, 2 + c), (down_hbm, down_buf, c))
     ):
         copy = remote(hbm.at[0, :, theirs], buf.at[slot], w_send_sem.at[k], w_recv_sem.at[k], twin)
         copy.start()
         sends.append(copy)
-
-    own_copies[0].wait()
-    own_copies[1].wait()
-    score_buf[...] = dot(cache_buf[...], q_buf[...]) * SCALE
-    visible = iota((CTX, HEADS), 0) < length_ref[0]
-    scores = jnp.where(visible, score_buf[...], -1e30)
-    highest = jnp.max(scores, axis=0, keepdims=True)
-    weights = jnp.where(visible, jnp.exp(scores - highest), 0.0)
-    prob_buf[...] = (weights / jnp.sum(weights, axis=0, keepdims=True)).astype(BF16)
 
     column = iota((128, 256), 0)
     col_j = column & 7
@@ -158,72 +154,80 @@
 
     pre_mid[...] = jnp.zeros_like(pre_mid)
 
-    for o in (1, 3, 2):
-        slot = z_buf.at[b, lax.rem(a - o + 4, 4)]
-        remote(slot, slot, z1_send.at[o - 1], z1_recv.at[o - 1], at_z(4 * o)).wait_recv()
-        hand_on(o)
-
-    context_ref[...] = dot(prob_buf[...], cache_buf[:, :LATENT], TN).astype(BF16)
-
-    for o in (0, 1, 3, 2):
-        for k, step in enumerate(near_steps):
-            plane = lax.rem(g - step + NZ, NZ)
-            slot = z_buf.at[plane % 4, lax.rem(plane // 4 - o + 4, 4)]
-            remote(slot, slot, z2_send.at[k, o], z2_recv.at[k, o], at_z(step)).wait_recv()
-    gathered = z_buf[...].reshape(256, PIECE)
-    found = dot(expert_pick, gathered[:, :128], NT)
-    found = jnp.where(row_j == PIECES, found, 0.0)
-    taken = onehot(found > 0)
-    slot_gate = dot(found.astype(BF16), spread)
-    standing = dot(taken, before)
-    chosen = (slot_gate > 0) & (standing == wanted_standing) & right_piece
-    place = onehot(chosen)
-    place_buf[...] = jnp.where(chosen, slot_gate, 0.0)
-    x_send[...] = dot(place, gathered).astype(BF16).reshape(PEERS, 16, PIECE)
-    for o in range(1, PEERS):
-        to = lax.rem(me + o, PEERS)
-        copy = remote(x_send.at[to], x_recv.at[me], x_ssem.at[o - 1], x_rsem.at[o - 1], peer(to))
-        copy.start()
-        sends.append(copy)
-    x_recv[me] = x_send[me]
-
-    for o in range(1, PEERS):
-        slot = x_recv.at[lax.rem(me - o + PEERS, PEERS)]
-        remote(slot, slot, x_ssem.at[o - 1], x_rsem.at[o - 1], peer(lax.rem(me + o, PEERS))).wait_recv()
-    y_buf[0] = dot(order, x_recv[...].reshape(128, PIECE)).astype(BF16).reshape(HALF, ROWS, PIECE)
+    for q in range(2):
+        for o in (1, 3, 2):
+            slot = z_buf.at[q, b, lax.rem(a - o + 4, 4)]
+            remote(slot, slot, z1_send.at[q, o - 1], z1_recv.at[q, o - 1], at_z(4 * o)).wait_recv()
+            hand_on(q, o)
+
+    for q in range(2):
+        for o in (0, 1, 3, 2):
+            for k, step in enumerate(near_steps):
+                plane = lax.rem(g - step + NZ, NZ)
+                slot = z_buf.at[q, plane % 4, lax.rem(plane // 4 - o + 4, 4)]
+                remote(slot, slot, z2_send.at[q, k, o], z2_recv.at[q, k, o], at_z(step)).wait_recv()
+        gathered = z_buf[q].reshape(256, LANES)
+        if q == 0:
+            found = dot(expert_pick, gathered[:, :128], NT)
+            found = jnp.where(row_j == PIECES, found, 0.0)
+            taken = onehot(found > 0)
+            slot_gate = dot(found.astype(BF16), spread)
+            standing = dot(taken, before)
+            chosen = (slot_gate > 0) & (standing == wanted_standing) & right_piece
+            place = onehot(chosen)
+            place_buf[...] = jnp.where(chosen, slot_gate, 0.0)
+        x_send[q] = dot(place, gathered).astype(BF16).reshape(PEERS, 16, LANES)
+        for o in range(1, PEERS):
+            to = lax.rem(me + o, PEERS)
+            copy = remote(x_send.at[q, to], x_recv.at[q, me], x_ssem.at[q, o - 1], x_rsem.at[q, o - 1], peer(to))
+            copy.start()
+            sends.append(copy)
+        x_recv[q, me] = x_send[q, me]
 
     def place_of(way, s):
         return 7 if s == 4 else 0 if s == 0 else 2 * s - 1 + way
 
-    def gather(way, s, j):
+    def gather(way, s, q, part):
+        first, last = GROUPS[part]
+        pieces = pl.ds(first, last - first)
         return remote(
-            y_buf.at[place_of(way, s - 1), j], y_buf.at[place_of(way, s), j],
-            y_ssem.at[way, s - 1, j], y_rsem.at[way, s - 1, j], at_y(1 - 2 * way),
+            y_buf.at[place_of(way, s - 1), q, pieces], y_buf.at[place_of(way, s), q, pieces],
+            y_ssem.at[way, s - 1, q, part], y_rsem.at[way, s - 1, q, part], at_y(1 - 2 * way),
         )
 
-    def gather_wait(way, s, j):
-        slot = y_buf.at[place_of(way, s), j]
-        remote(slot, slot, y_ssem.at[way, s - 1, j], y_rsem.at[way, s - 1, j], at_y(1 - 2 * way)).wait_recv()
-
-    def weight_piece(j):
-        return gu_buf[:, :, j * PIECE : (j + 1) * PIECE].reshape(4 * HID, PIECE)
+    def gather_wait(way, s, q, part):
+        first, last = GROUPS[part]
+        slot = y_buf.at[place_of(way, s), q, pl.ds(first, last - first)]
+        ssem, rsem = y_ssem.at[way, s - 1, q, part], y_rsem.at[way, s - 1, q, part]
+        remote(slot, slot, ssem, rsem, at_y(1 - 2 * way)).wait_recv()
+
+    def weight_piece(q, j):
+        first = j * PIECE + q * LANES
+        return gu_buf[:, :, first : first + LANES].reshape(4 * HID, LANES)
 
     last_way = [0] * GROUPS[0][1] + [1] * (HALF - GROUPS[0][1])
 
-    def steps_of(s):
-        return [(way, j) for j in range(HALF) for way in range(2) if s < 4 or last_way[j] == way]
-
-    for way, j in steps_of(1):
-        copy = gather(way, 1, j)
-        copy.start()
-        sends.append(copy)
+    def steps_of(s, q):
+        return [(way, q, part) for part in range(2) for way in range(2) if s < 4 or part == way]
+
+    for q in range(2):
+        for o in range(1, PEERS):
+            slot = x_recv.at[q, lax.rem(me - o + PEERS, PEERS)]
+            to = peer(lax.rem(me + o, PEERS))
+            remote(slot, slot, x_ssem.at[q, o - 1], x_rsem.at[q, o - 1], to).wait_recv()
+        y_buf[0, q] = dot(order, x_recv[q].reshape(128, LANES)).astype(BF16).reshape(HALF, ROWS, LANES)
+        for chunk in steps_of(1, q):
+            copy = gather(chunk[0], 1, *chunk[1:])
+            copy.start()
+            sends.append(copy)
     for s in range(1, 4):
-        for way, j in steps_of(s):
-            gather_wait(way, s, j)
-            if (way, j) in steps_of(s + 1):
-                copy = gather(way, s + 1, j)
-                copy.start()
-                sends.append(copy)
+        for q in range(2):
+            for way, _, part in steps_of(s, q):
+                gather_wait(way, s, q, part)
+                if s < 3 or part == way:
+                    copy = gather(way, s + 1, q, part)
+                    copy.start()
+                    sends.append(copy)
         if s == 1:
             for copy in own_copies[2:]:
                 copy.wait()
@@ -233,17 +237,20 @@
         if s == 3:
             rows = 7 * ROWS
             total = jnp.zeros((4 * HID, rows), F32)
-            for j in range(HALF):
-                total += dot(weight_piece(j), y_buf[:7, j].reshape(rows, PIECE), NT)
+            for q in range(2):
+                for j in range(HALF):
+                    total += dot(weight_piece(q, j), y_buf[:7, q, j].reshape(rows, LANES), NT)
             pre_mid[:, :rows] = total
             mid = remote(pre_mid, mid_recv, p_ssem.at[0], p_rsem.at[0], twin)
             mid.start()
             sends.append(mid)
-    for way, j in steps_of(4):
-        gather_wait(way, 4, j)
+    for q in range(2):
+        for way, _, part in steps_of(4, q):
+            gather_wait(way, 4, q, part)
     total = jnp.zeros((ROWS, 4 * HID), F32)
-    for j in range(HALF):
-        total += dot(y_buf[7, j], weight_piece(j), NT)
+    for q in range(2):
+        for j in range(HALF):
+            total += dot(y_buf[7, q, j], weight_piece(q, j), NT)
     pre_end[...] = total
     end = remote(pre_end, end_recv, p_ssem.at[1], p_rsem.at[1], twin)
     end.start()
@@ -306,6 +313,15 @@
         copy.start()
         sends.append(copy)
     b_recv[me] = b_send[me]
+    own_copies[0].wait()
+    own_copies[1].wait()
+    score_buf[...] = dot(cache_buf[...], q_buf[...]) * SCALE
+    visible = iota((CTX, HEADS), 0) < length_ref[0]
+    scores = jnp.where(visible, score_buf[...], -1e30)
+    highest = jnp.max(scores, axis=0, keepdims=True)
+    weights = jnp.where(visible, jnp.exp(scores - highest), 0.0)
+    prob_buf[...] = (weights / jnp.sum(weights, axis=0, keepdims=True)).astype(BF16)
+
     weigh = place_buf[...].T.astype(BF16)
     for o in range(1, PEERS):
         slot = b_recv.at[lax.rem(me - o + PEERS, PEERS)]
@@ -321,6 +337,8 @@
             )
             copy.start()
             sends.append(copy)
+    context_ref[...] = dot(prob_buf[...], cache_buf[:, :LATENT], TN).astype(BF16)
+
     for o in (2, 1, 3, 0):
         total = c_buf[b, lax.rem(a + o, 4)].astype(F32)
         for k in range(3):
@@ -359,11 +377,11 @@
             pltpu.VMEM((CTX, HEADS), BF16),
             pltpu.VMEM((4, HID, HALF_D), BF16),
             pltpu.VMEM((2, HID, HALF_D), BF16),
-            pltpu.VMEM((4, 4, 16, PIECE), BF16),
+            pltpu.VMEM((2, 4, 4, 16, LANES), BF16),
             pltpu.VMEM((128, 256), F32),
-            pltpu.VMEM((PEERS, 16, PIECE), BF16),
-            pltpu.VMEM((PEERS, 16, PIECE), BF16),
-            pltpu.VMEM((NY, HALF, ROWS, PIECE), BF16),
+            pltpu.VMEM((2, PEERS, 16, LANES), BF16),
+            pltpu.VMEM((2, PEERS, 16, LANES), BF16),
+            pltpu.VMEM((NY, 2, HALF, ROWS, LANES), BF16),
             pltpu.VMEM((4 * HID, 128), F32),
             pltpu.VMEM((4 * HID, 128), F32),
             pltpu.VMEM((ROWS, 4 * HID), F32),
@@ -377,18 +395,17 @@
             pltpu.VMEM((3, 4, 16, PIECE), BF16),
             pltpu.VMEM((3, 16, PIECE), BF16),
             pltpu.VMEM((3, 16, PIECE), BF16),
-            pltpu.VMEM((2880, 8192), BF16),
             dma((5,)), dma((3,)), dma((3,)),
-            dma((3,)), dma((3,)), dma((3, 4)), dma((3, 4)),
-            dma((7,)), dma((7,)),
-            dma((2, 4, 7)), dma((2, 4, 7)),
+            dma((2, 3)), dma((2, 3)), dma((2, 3, 4)), dma((2, 3, 4)),
+            dma((2, 7)), dma((2, 7)),
+            dma((2, 4, 2, 2)), dma((2, 4, 2, 2)),
             dma((2,)), dma((2,)),
             dma((2, 4, 7)), dma((2, 4, 7)),
             dma((7,)), dma((7,)),
             dma((3, 4)), dma((3, 4)), dma((3,)), dma((3,)),
         ],
         compiler_params=pltpu.CompilerParams(
-            collective_id=0, has_side_effects=True, vmem_limit_bytes=60 * 1024 * 1024
+            collective_id=0, has_side_effects=True, vmem_limit_bytes=55000 * 1024
         ),
         cost_estimate=pl.CostEstimate(flops=1_000_000_000, bytes_accessed=4_000_000, transcendentals=50_000),
     )(lengths, moe_rows, expert_ids, route_gates, jnp.swapaxes(queries, 1, 2), latent_cache, w_gate, w_up, w_down)

time: 92.8 us -> 91.3 us (0.984)
  the two profiles are of different devices: /device:TPU:4 before, /device:TPU:8 now
where the time goes in v3:
time: 91.3 us; the launch traced here: 91.1 us
  Pallas kernels  87.1 us (95%)
  local copies, waits for them, and re-layouts  2.67 us (3%)
  between operations  1.3 us (1%)
    pallas_call x1, Pallas kernels, per_device(): pl.pallas_call(kernel, out_shape=(jax.ShapeDtypeStruct((HEADS, LATENT), B...  87.1 us
    unnamed x8, local copies, waits for them, and re-layouts  2.67 us

profile of v3, /device:TPU:8, one launch (start us, length us, event | category | flops | bytes accessed | tf_op | source)
XLA Modules:
  0.0 91.1 jit_solution(6314486301623945971)
XLA Ops:
  1.3 0.0 copy-start.1
  1.3 0.0 copy-start.2
  1.3 0.6 copy-done.1
  1.9 0.0 copy-done.2
  1.9 0.0 copy-start
  2.0 0.7 copy-done
  2.7 87.1 %shard_map.104 = (bf16[128,512]{1,0:T(8,128)(2,1)S(1)}, bf16[1,7168]{1,0:T(2,128)(2,1)S(1)}) custom-call(s32[1]{0:T(128)S(6)} %copy.13.length_ref, bf16[1,7168]{1,0:T(2,128)(2,1)S(1)} %copy-done, s32[1,8]{1,0:T(1,128)S(1)} %copy-done.1, bf16[1,8]{1,0:T(2,128)(2,1)S(1)} %copy-done.2, bf16[1,576,128]{2,1,0:T(8,128)(2,1)} %bitcast.3, ...), custom_call_target="tpu_custom_call" | custom-call | flops 1000000000 | bytes 4000000 | tf_op jit(solution)/shard_map/pallas_call | solution.py:365
  89.8 0.7 copy.14
  90.4 0.6 copy.15
Async XLA Ops:
  1.3 0.7 copy-start.1
  1.3 0.7 copy-start.2
  1.9 0.7 copy-start
